TPU v7x, 32 devices: a whole 2x2x4 slice. The times are simulated.
32 devices in a mesh: groups: 2 (over y), blk: 4 (over z), inner: 4 (over x, core).
Axes of the slice: x: 2, y: 2, z: 4, core: 2. Of those that a mesh axis runs over, the one named last changes fastest.
Arguments:
- points: float32 [8192, 64], P(('groups', 'blk', 'inner')), parts along dimension 0, may hold values from -6 to 6
- inverse_scale: float32 [128], P('groups'), parts along dimension 0, may hold values from 0.125 to 0.375
- noise_var: float32 [8192], P(('groups', 'blk', 'inner')), parts along dimension 0, may hold values from 0.1 to 1
- solution: float32 [8192, 32], P(('groups', 'blk', 'inner')), parts along dimension 0, may hold values from -6 to 6
- residual: float32 [8192, 32], P(('groups', 'blk', 'inner')), parts along dimension 0, may hold values from -6 to 6
- direction: float32 [8192, 32], P(('groups', 'blk', 'inner')), parts along dimension 0, may hold values from -6 to 6
Outputs:
- solution_next: float32 [8192, 32], P(('groups', 'blk', 'inner')), parts along dimension 0
- residual_next: float32 [8192, 32], P(('groups', 'blk', 'inner')), parts along dimension 0
- direction_next: float32 [8192, 32], P(('groups', 'blk', 'inner')), parts along dimension 0
There are 2 independent parts, one for each index of `groups`. A program takes and returns all parts, laid end to end along the dimension named above; each array names one. Nothing has to cross between parts.
All inputs are finite; a program needn't handle non-finite values.
Results may differ from a plain program's by a relative error of at most 0.0003.
Values sent between devices are 32-bit elements; how exact they have to be, the bound alone decides.
A program may use at most 64 MiB of HBM per device.

v0:
```python
import math

import jax
import jax.numpy as jnp
from jax import lax
from jax.sharding import PartitionSpec as P


def matern(sq):
    root = jnp.sqrt(5.0 * jnp.maximum(sq, 0.0))
    return (1.0 + root + root * root / 3.0) * jnp.exp(-root)


def make_folder(rows_z, total, piece):
    high = lax.Precision.HIGHEST
    rows_n = jnp.sum(rows_z * rows_z, axis=1)
    feats = rows_z.shape[1]
    tile_cols = max(128, 524288 // rows_z.shape[0])
    cols_z, cols_p = piece
    count = cols_z.shape[0]
    width = math.gcd(count, tile_cols)
    z_blocks = cols_z.reshape(count // width, width, feats)
    p_blocks = cols_p.reshape(count // width, width, cols_p.shape[1])

    def step_block(acc, pair):
        block_z, block_p = pair
        block_n = jnp.sum(block_z * block_z, axis=1)
        cross = jnp.dot(rows_z, block_z.T, precision=high)
        sq = rows_n[:, None] + block_n[None, :] - 2.0 * cross
        return (acc + jnp.dot(matern(sq), block_p, precision=high), None)

    result, unused = lax.scan(step_block, total, (z_blocks, p_blocks))
    return result


def shards(points, inverse_scale, noise_var, solution, residual, direction):
    high = lax.Precision.HIGHEST
    scaled = points * inverse_scale
    columns = direction.shape[1]
    block_rows = lax.all_gather(scaled, "inner", axis=0, tiled=True)
    start_sum = jnp.zeros((block_rows.shape[0], columns), jnp.float32)
    partial_sum = make_folder(
        block_rows,
        start_sum,
        (
            lax.all_gather(scaled, "blk", axis=0, tiled=True),
            lax.all_gather(direction, "blk", axis=0, tiled=True),
        ),
    )
    image = lax.psum_scatter(partial_sum, "inner", scatter_dimension=0, tiled=True)
    image = image + noise_var[:, None] * direction
    local_curv = jnp.dot(direction.T, image, precision=high)
    local_gram = jnp.dot(residual.T, residual, precision=high)
    curv, gram = lax.psum((local_curv, local_gram), ("blk", "inner"))
    alpha = jax.scipy.linalg.cho_solve((jnp.linalg.cholesky(curv), True), gram)
    residual_next = residual - jnp.dot(image, alpha, precision=high)
    gram_next = lax.psum(jnp.dot(residual_next.T, residual_next, precision=high), ("blk", "inner"))
    solution_next = solution + jnp.dot(direction, alpha, precision=high)
    beta = jax.scipy.linalg.cho_solve((jnp.linalg.cholesky(gram), True), gram_next)
    direction_next = residual_next + jnp.dot(direction, beta, precision=high)
    return (solution_next, residual_next, direction_next)


def solution(mesh):
    in_specs = (
        P(("groups", "blk", "inner"), None),
        P("groups"),
        P(("groups", "blk", "inner")),
        P(("groups", "blk", "inner"), None),
        P(("groups", "blk", "inner"), None),
        P(("groups", "blk", "inner"), None),
    )
    out_specs = (
        P(("groups", "blk", "inner"), None),
        P(("groups", "blk", "inner"), None),
        P(("groups", "blk", "inner"), None),
    )
    return jax.shard_map(shards, mesh=mesh, in_specs=in_specs, out_specs=out_specs, check_vma=False)
```

profile of v0, /device:TPU:0, one launch (start us, length us, event | category | flops | bytes accessed | tf_op | source)
XLA Modules:
  0.0 223.4 jit_solution(17867362142194807215)
XLA Ops:
  7.2 0.9 copy.9
  8.2 0.7 broadcast_multiply_fusion
  8.8 8.6 %all_gather.9 = f32[1024,64]{1,0:T(8,128)S(1)} all-gather(f32[256,64]{1,0:T(8,128)S(1)} %broadcast_multiply_fusion), channel_id=1, replica_groups=mesh['groups'=2,'blk'=4,'inner'=4] {'inner'}, dimensions={0}, use_global_device_ids=true | all-gather | bytes 327680 | tf_op jit(solution)/shard_map/all_gather | solution.py:40
  17.4 16.3 %all_gather.10 = f32[1024,64]{1,0:T(8,128)S(1)} all-gather(f32[256,64]{1,0:T(8,128)S(1)} %broadcast_multiply_fusion), channel_id=1, replica_groups=mesh['groups'=2,'blk'=4,'inner'=4] {'blk'}, dimensions={0}, use_global_device_ids=true | all-gather | bytes 327680 | tf_op jit(solution)/shard_map/all_gather | solution.py:46
  34.0 13.4 %all_gather.11 = f32[1024,32]{0,1:T(8,128)S(1)} all-gather(f32[256,32]{0,1:T(8,128)S(1)} %copy-done), channel_id=1, replica_groups=mesh['groups'=2,'blk'=4,'inner'=4] {'blk'}, dimensions={0}, use_global_device_ids=true | all-gather | bytes 163840 | tf_op jit(solution)/shard_map/all_gather | solution.py:47
  47.4 1.0 copy.10
  48.4 11.3 %while.11 = (s32[]{:T(128)}, f32[1024,32]{0,1:T(8,128)S(1)}, f32[1024]{0:T(1024)S(1)}, f32[2,512,64]{2,1,0:T(8,128)S(1)}, f32[1024,64]{1,0:T(8,128)S(1)}, /*index=5*/f32[2,512,32]{2,1,0:T(8,128)}, s32[]{:T(128)}, s32[]{:T(128)}) while((s32[]{:T(128)}, f32[1024,32]{0,1:T(8,128)S(1)}, f32[1024]{0:T(1024)S(1)}, ...), condition=%wide.region_3.4_spmd.clone, body=%wide.region_1.3_spmd.clone.sunk | while | flops 609877504 | bytes 5644903 | solution.py:32
  48.4 1.8 fusion.81
  50.4 3.7 %fusion.83 = f32[1024,32]{0,1:T(8,128)S(1)} fusion(f32[512,1024]{1,0:T(8,128)S(1)} %fusion.81, f32[512]{0:T(512)S(1)} %fusion.82, f32[1024]{0:T(1024)S(1)} %get-tuple-element.130, f32[2,512,32]{2,1,0:T(8,128)} %get-tuple-element.133, s32[]{:T(128)} %get-tuple-element.120, f32[1024,32]{0,1:T(8,128)S(1)} %get-tuple-element.121, pred[]{:T(512)S(6)} %compare.13), kind=kOutput, calls=%fused_computation.14.clone.1 | convolution fusion | flops 207159296 | bytes 2628097 | tf_op jit(solution)/shard_map/while/body/eval_jaxpr/dot_general | solution.py:30
  54.0 1.8 fusion.81
  56.0 3.7 %fusion.83 = f32[1024,32]{0,1:T(8,128)S(1)} fusion(f32[512,1024]{1,0:T(8,128)S(1)} %fusion.81, f32[512]{0:T(512)S(1)} %fusion.82, f32[1024]{0:T(1024)S(1)} %get-tuple-element.130, f32[2,512,32]{2,1,0:T(8,128)} %get-tuple-element.133, s32[]{:T(128)} %get-tuple-element.120, f32[1024,32]{0,1:T(8,128)S(1)} %get-tuple-element.121, pred[]{:T(512)S(6)} %compare.13), kind=kOutput, calls=%fused_computation.14.clone.1 | convolution fusion | flops 207159296 | bytes 2628097 | tf_op jit(solution)/shard_map/while/body/eval_jaxpr/dot_general | solution.py:30
  60.5 20.5 %reduce-scatter.2.cloned.1.call-done = f32[256,32]{0,1:T(8,128)} async-done(((f32[1024,32]{0,1:T(8,128)}), f32[256,32]{0,1:T(8,128)}) %reduce-scatter.2.cloned.1.call-update) | async-done | bytes 32784 | tf_op jit(solution)/shard_map/reduce_scatter | solution.py:50
  81.1 0.9 convolution_bitcast_fusion.2
  82.0 59.8 %all-reduce = (f32[32,32]{0,1:T(8,128)S(1)}, f32[32,32]{0,1:T(8,128)S(1)}) all-reduce(f32[32,32]{0,1:T(8,128)S(1)} %fusion.53, f32[32,32]{0,1:T(8,128)S(1)} %convolution_bitcast_fusion.2), channel_id=1, replica_groups=mesh['groups'=2,'blk'=4,'inner'=4] {'blk','inner'}, use_global_device_ids=true, to_apply=%region_8.10 | all-reduce | flops 2048 | bytes 16384 | tf_op jit(solution)/shard_map/psum | solution.py:54
  141.9 2.9 %cholesky.55 = f32[32,32]{1,0:T(8,128)S(1)} custom-call(f32[32,32]{1,0:T(8,128)S(1)} %get-tuple-element.73), custom_call_target="Cholesky" | custom-call | tf_op jit(solution)/shard_map/jit(cholesky)/cholesky | solution.py:59
  145.5 0.7 fusion.40
  146.2 2.4 %custom-call.10 = f32[1,32,32]{1,2,0:T(8,128)S(1)} custom-call(f32[1,32,32]{2,1,0:T(8,128)S(1)} %fusion.40), custom_call_target="InvertDiagBlocksLowerTriangular" | custom-call | tf_op jit(solution)/shard_map/jit(_cho_solve)/triangular_solve | solution.py:59
  148.6 2.9 %cholesky.44 = f32[32,32]{1,0:T(8,128)S(1)} custom-call(f32[32,32]{1,0:T(8,128)S(1)} %get-tuple-element.74), custom_call_target="Cholesky" | custom-call | tf_op jit(solution)/shard_map/jit(cholesky)/cholesky | solution.py:55
  152.3 0.7 fusion.39
  152.9 2.4 %custom-call.9 = f32[1,32,32]{1,2,0:T(8,128)S(1)} custom-call(f32[1,32,32]{2,1,0:T(8,128)S(1)} %fusion.39), custom_call_target="InvertDiagBlocksLowerTriangular" | custom-call | tf_op jit(solution)/shard_map/jit(_cho_solve)/triangular_solve | solution.py:55
  155.7 1.0 convolution_subtract_fusion
  156.9 57.6 %psum.23 = f32[32,32]{1,0:T(8,128)S(1)} all-reduce(f32[32,32]{1,0:T(8,128)S(1)} %fusion.54), channel_id=1, replica_groups=mesh['groups'=2,'blk'=4,'inner'=4] {'blk','inner'}, use_global_device_ids=true, to_apply=%region_9.12 | all-reduce | flops 1024 | bytes 8192 | tf_op jit(solution)/shard_map/psum | solution.py:57
  214.9 0.9 fusion.37
  215.7 0.8 fusion.38
  (31 shorter events, 3.7 us)
Async XLA Ops:
  7.2 26.8 %copy-start = (f32[256,32]{0,1:T(8,128)S(1)}, f32[256,32]{0,1:T(8,128)}, u32[]{:S(2)}) copy-start(f32[256,32]{0,1:T(8,128)} %param.16) | copy-start | bytes 98308
  7.2 73.9 %reduce-scatter.2.cloned.1.call-start = ((), (), s32[]{:S(2)}) async-start(), calls=%async_computation.1 | async-start | bytes 163840 | tf_op jit(solution)/shard_map/reduce_scatter | solution.py:50
  48.4 12.0 %copy-start.2 = (f32[256,32]{0,1:T(8,128)S(1)}, f32[256,32]{0,1:T(8,128)}, u32[]{:S(2)}) copy-start(f32[256,32]{0,1:T(8,128)} %param.15) | copy-start | bytes 98308
  48.4 32.7 %copy-start.5 = (f32[256]{0:T(256)S(1)}, f32[256]{0:T(256)}, u32[]{:S(2)}) copy-start(f32[256]{0:T(256)} %param.13) | copy-start | bytes 3076
  48.4 167.3 %copy-start.4 = (f32[256,32]{0,1:T(8,128)S(1)}, f32[256,32]{0,1:T(8,128)}, u32[]{:S(2)}) copy-start(f32[256,32]{0,1:T(8,128)} %param.14) | copy-start | bytes 98308
  59.7 0.6 copy-start.3
  156.7 59.8 %copy-start.1 = (f32[256,32]{0,1:T(8,128)}, f32[256,32]{0,1:T(8,128)S(1)}, u32[]{:S(2)}) copy-start(f32[256,32]{0,1:T(8,128)S(1)} %convolution_subtract_fusion) | copy-start | bytes 98308
Sparse Core Ops, SparseCore 0:
  60.5 20.5 reduce-scatter.1
where the time goes:
time: 224 us; the launch traced here: 223 us
  blocking collectives  156 us (70%)
  waiting for transfers between devices  20.6 us (9%)
  matrix products  15.5 us (7%)
  other arithmetic  14.6 us (7%)
  between operations  14.2 us (6%)
  local copies, waits for them, and re-layouts  2.72 us (1%)
    psum x1, blocking collectives, shards(): curv, gram = lax.psum((local_curv, local_gram), ('blk', 'inner'))  59.8 us
    psum x1, blocking collectives, shards(): lax.psum(jnp.dot(residual_next.T, residual_next, precision=high), ('blk',...  57.6 us
    reduce_scatter x1, waiting for transfers between devices, shards(): lax.psum_scatter(partial_sum, 'inner', scatter_dimension=0, tiled=True)  20.5 us
    all_gather x1, blocking collectives, shards(): lax.all_gather(scaled, 'blk', axis=0, tiled=True)  16.3 us
    all_gather x1, blocking collectives, shards(): lax.all_gather(direction, 'blk', axis=0, tiled=True)  13.4 us
    all_gather x1, blocking collectives, shards(): block_rows = lax.all_gather(scaled, 'inner', axis=0, tiled=True)  8.62 us
    dot_general x2, matrix products, step_block(): return (acc + jnp.dot(matern(sq), block_p, precision=high), None)  7.32 us
    another operation x5, other arithmetic, shards(): alpha = jax.scipy.linalg.cho_solve((jnp.linalg.cholesky(curv), True), gram)  6.7 us
  transfers between devices with their start and end apart: 1, of which 1 were waited for; matrix products, arithmetic and copies ran while one was open for 0% of the time, Pallas kernels for 0%

commit v1 on v0

v1 whole, which is shorter than its diff:
```python
import functools
import math

import jax
import jax.numpy as jnp
from jax import lax
from jax.experimental import pallas as pl
from jax.experimental.pallas import tpu as pltpu
from jax.sharding import PartitionSpec as P

MESH = pl.DeviceIdType.MESH
HIGH = lax.Precision.HIGHEST
LN2 = math.log(2.0)
FEATURE_SCALE = math.sqrt(5.0) / LN2
f32 = jnp.float32
bf16 = jnp.bfloat16


def dot(a, b, ca, cb, precision=HIGH):
    return lax.dot_general(a, b, (((ca,), (cb,)), ((), ())), precision=precision, preferred_element_type=f32)


def lanes(shape):
    return lax.broadcasted_iota(jnp.int32, shape, len(shape) - 1)


def halves(packed):
    hi = packed.astype(bf16).astype(f32)
    lo = (packed - hi).astype(bf16).astype(f32)
    return hi, lo


def row_operand(packed):
    hi, lo = halves(packed)
    left = lanes(packed.shape) < 64
    lo_r = pltpu.roll(lo, 64, 1)
    top = jnp.where(left, hi, lo_r) * -2.0
    low = jnp.where(left, lo_r, hi) * -2.0
    both = jnp.concatenate([top, low], axis=0).astype(bf16)
    sq = (hi + lo) * (hi + lo)
    n_top = jnp.sum(jnp.where(left, sq, 0.0), axis=1, keepdims=True)
    n_low = jnp.sum(jnp.where(left, 0.0, sq), axis=1, keepdims=True)
    norms = jnp.concatenate([n_top, n_low], axis=0)
    return jnp.concatenate([both, both], axis=1), norms


def col_operand(packed):
    hi, lo = halves(packed)
    left = lanes(packed.shape) < 64
    hi_r, lo_r = pltpu.roll(hi, 64, 1), pltpu.roll(lo, 64, 1)
    hh = jnp.concatenate([jnp.where(left, hi, hi_r), jnp.where(left, hi_r, hi)], axis=0)
    ll = jnp.concatenate([jnp.where(left, lo, lo_r), jnp.where(left, lo_r, lo)], axis=0)
    sq = (hi + lo) * (hi + lo)
    pick = lanes((8, 128)) < 64
    n_top = dot(jnp.where(pick, 1.0, 0.0), sq, 1, 1)
    n_low = dot(jnp.where(pick, 0.0, 1.0), sq, 1, 1)
    return (
        jnp.concatenate([hh, ll], axis=1).astype(bf16),
        jnp.concatenate([n_top, n_low], axis=1),
    )


def pack4(x):
    n = x.shape[0] // 4
    return jnp.concatenate([x[g * n:(g + 1) * n] for g in range(4)], axis=1)


def unpack4(x):
    return jnp.concatenate([x[:, g * 32:(g + 1) * 32] for g in range(4)], axis=0)


def spread4(packed):
    group = lanes(packed.shape) // 32
    out = []
    for g in range(4):
        m = jnp.where(group == g, packed, 0.0)
        m = m + pltpu.roll(m, 64, 1)
        out.append(m + pltpu.roll(m, 32, 1))
    return jnp.concatenate(out, axis=0)


def dir_operand(packed):
    d = spread4(packed)
    hi, lo = halves(d)
    return jnp.where((lanes(d.shape) // 32) % 2 == 0, hi, lo).astype(bf16)


def eliminate(systems):
    n = systems[0].shape[0]
    rows = lax.broadcasted_iota(jnp.int32, (n, 1), 0)
    for k in range(n):
        done = []
        for a in systems:
            pivot = a[k:k + 1, :] / a[k:k + 1, k:k + 1]
            column = jnp.where(rows == k, 0.0, a[:, k:k + 1])
            done.append(jnp.where(rows == k, pivot, a - column * pivot))
        systems = done
    return [a[:, n:2 * n] for a in systems]


def kernel(nb, ni, points_ref, scale_ref, noise_ref, sol_ref, res_ref, dir_ref, sol_out, res_out, dir_out,
           wrow, cols, a_op, rn, b_op, cn, d_op, acc, parts, sums_i, sums_b,
           w_send, w_recv, c_right, c_left, c_recv, p_send, p_recv, si_send, si_recv, sb_send, sb_recv):
    n = points_ref.shape[0]
    h, q = n // 2, n // 4
    b = lax.axis_index("blk")
    i = lax.axis_index("inner")

    barrier = pltpu.get_barrier_semaphore()
    for off in range(1, ni):
        pl.semaphore_signal(barrier, inc=1, device_id={"inner": lax.rem(i + off, ni)}, device_id_type=MESH)

    @pl.loop(1, nb)
    def _(off):
        pl.semaphore_signal(barrier, inc=1, device_id={"blk": lax.rem(b + off, nb)}, device_id_type=MESH)

    w = points_ref[...] * (scale_ref[...] * FEATURE_SCALE)
    packed_w = jnp.concatenate([w[:h], w[h:]], axis=1)
    wrow[i] = packed_w
    cols[b, :h] = packed_w
    cols[b, h:] = pack4(dir_ref[...])
    pl.semaphore_wait(barrier, ni + nb - 2)

    def w_copy(src, to):
        return pltpu.make_async_remote_copy(
            src_ref=wrow.at[src], dst_ref=wrow.at[src], send_sem=w_send.at[to], recv_sem=w_recv.at[src],
            device_id={"inner": to}, device_id_type=MESH)

    def c_copy(owner, to, sems):
        return pltpu.make_async_remote_copy(
            src_ref=cols.at[owner], dst_ref=cols.at[owner], send_sem=sems.at[owner], recv_sem=c_recv.at[owner],
            device_id={"blk": to}, device_id_type=MESH)

    @pl.when(b + 1 < nb)
    def _():
        c_copy(b, b + 1, c_right).start()

    @pl.when(b >= 1)
    def _():
        c_copy(b, b - 1, c_left).start()

    for off in range(1, ni):
        w_copy(i, lax.rem(i + off, ni)).start()

    r = res_ref[...]
    zero = jnp.zeros((n, 32), f32)
    gram_part = dot(r, jnp.concatenate([zero, zero, zero, r], axis=1), 0, 0)
    eye = lax.broadcasted_iota(jnp.int32, (n, n), 0) == lax.broadcasted_iota(jnp.int32, (n, n), 1)
    noise = jnp.sum(jnp.where(eye, noise_ref[...], 0.0), axis=1, keepdims=True)
    acc[...] = jnp.zeros_like(acc)

    def prepare(j):
        op, norms = row_operand(wrow[j])
        a_op[j] = op
        rn[j] = jnp.broadcast_to(norms, (n, 128))

    prepare(i)
    for off in range(1, ni):
        src = lax.rem(i - off + ni, ni)
        w_copy(src, src).wait_recv()
        prepare(src)

    reach = jnp.minimum(b, nb - 1 - b)

    @pl.loop(0, nb)
    def _(t):
        near = (t + 1) // 2
        paired = b + near * (1 - 2 * (t % 2))
        far = t - reach
        single = jnp.where(2 * b > nb - 1, b - far, b + far)
        owner = jnp.where(t <= 2 * reach, paired, single)

        @pl.when(t > 0)
        def _():
            c_copy(owner, b, c_right).wait_recv()

            @pl.when(jnp.logical_and(owner < b, b + 1 < nb))
            def _():
                c_copy(owner, b + 1, c_right).start()

            @pl.when(jnp.logical_and(owner > b, b >= 1))
            def _():
                c_copy(owner, b - 1, c_left).start()

        op, norms = col_operand(cols[owner, :h])
        b_op[...] = op
        cn[...] = norms
        d_op[...] = dir_operand(cols[owner, h:])

        @pl.loop(0, ni)
        def _(j):
            cross = dot(a_op[j], b_op[...], 1, 1, None)
            row_n = rn[j]
            x = cross + jnp.concatenate([row_n] * (n // 128), axis=1) + cn[0:1, :]
            x = jnp.maximum(x, 1e-30)
            v = x * lax.rsqrt(x)
            k = (1.0 + LN2 * v + (LN2 * LN2 / 3.0) * x) * jnp.exp2(-v)
            kh = k.astype(bf16)
            kl = (k - kh.astype(f32)).astype(bf16)
            acc[j] += dot(kh, d_op[...], 1, 0, None) + dot(kl, d_op[...], 1, 0, None)

    group = lanes((q, 128)) // 32

    def packed_part(j):
        a = acc[j]
        a = a + pltpu.roll(a, 32, 1)
        out = a[:q]
        for g in range(1, 4):
            out = jnp.where(group == g, a[g * q:(g + 1) * q], out)
        return out

    def p_copy(to, src):
        return pltpu.make_async_remote_copy(
            src_ref=parts.at[0, to], dst_ref=parts.at[1, src], send_sem=p_send.at[to], recv_sem=p_recv.at[src],
            device_id={"inner": to}, device_id_type=MESH)

    for off in range(1, ni):
        to = lax.rem(i + off, ni)
        parts[0, to] = packed_part(to)
        p_copy(to, i).start()
    image = packed_part(i)
    for off in range(1, ni):
        src = lax.rem(i - off + ni, ni)
        p_copy(src, src).wait_recv()
        image = image + parts[1, src]
    d = dir_ref[...]
    image = unpack4(image) + noise * d

    total = dot(image, jnp.concatenate([d, r, image, zero], axis=1), 0, 0) + gram_part

    def s_copy(buf, me, to, src, send, recv, axis):
        return pltpu.make_async_remote_copy(
            src_ref=buf.at[me], dst_ref=buf.at[src], send_sem=send.at[to], recv_sem=recv.at[src],
            device_id={axis: to}, device_id_type=MESH)

    sums_i[i] = total
    for off in range(1, ni):
        s_copy(sums_i, i, lax.rem(i + off, ni), i, si_send, si_recv, "inner").start()
    for off in range(1, ni):
        src = lax.rem(i - off + ni, ni)
        s_copy(sums_i, i, src, src, si_send, si_recv, "inner").wait_recv()
    total = sums_i[0]
    for j in range(1, ni):
        total = total + sums_i[j]
    sums_b[b] = total

    @pl.loop(1, nb)
    def _(off):
        s_copy(sums_b, b, lax.rem(b + off, nb), b, sb_send, sb_recv, "blk").start()

    @pl.loop(1, nb)
    def _(off):
        src = lax.rem(b - off + nb, nb)
        s_copy(sums_b, b, src, src, sb_send, sb_recv, "blk").wait_recv()

    total = lax.fori_loop(1, nb, lambda j, s: s + sums_b[j], sums_b[0])

    curv, qr, qq, gram = [total[:, 32 * g:32 * g + 32] for g in range(4)]
    curv = 0.5 * (curv + curv.T)
    unit = (lax.broadcasted_iota(jnp.int32, (32, 32), 0) == lax.broadcasted_iota(jnp.int32, (32, 32), 1)).astype(f32)
    alpha, gram_inv = eliminate([jnp.concatenate([curv, gram], axis=1), jnp.concatenate([gram, unit], axis=1)])
    change = qr - dot(qq, alpha, 1, 0)
    gram_next = gram - dot(qr, alpha, 0, 0) - dot(alpha, change, 0, 0)
    beta = dot(gram_inv, gram_next, 1, 0)
    r_next = r - dot(image, alpha, 1, 0)
    res_out[...] = r_next
    sol_out[...] = sol_ref[...] + dot(d, alpha, 1, 0)
    dir_out[...] = r_next + dot(d, beta, 1, 0)

    for off in range(1, ni):
        to = lax.rem(i + off, ni)
        w_copy(i, to).wait_send()
        p_copy(to, i).wait_send()
        s_copy(sums_i, i, to, i, si_send, si_recv, "inner").wait_send()

    @pl.loop(1, nb)
    def _(off):
        s_copy(sums_b, b, lax.rem(b + off, nb), b, sb_send, sb_recv, "blk").wait_send()

    @pl.loop(0, nb)
    def _(o):
        @pl.when(jnp.logical_and(o <= b, b + 1 < nb))
        def _():
            c_copy(o, b, c_right).wait_send()

        @pl.when(jnp.logical_and(o >= b, b >= 1))
        def _():
            c_copy(o, b, c_left).wait_send()


def solution(mesh):
    nb, ni = mesh.shape["blk"], mesh.shape["inner"]

    def shards(points, inverse_scale, noise_var, sol, residual, direction):
        n, feats = points.shape
        columns = direction.shape[1]
        dma = lambda k: pltpu.SemaphoreType.DMA((k,))
        vmem = pl.BlockSpec(memory_space=pltpu.VMEM)
        out = jax.ShapeDtypeStruct((n, columns), f32)
        return pl.pallas_call(
            functools.partial(kernel, nb, ni),
            out_shape=(out, out, out),
            in_specs=[vmem] * 6,
            out_specs=(vmem, vmem, vmem),
            scratch_shapes=[
                pltpu.VMEM((ni, n // 2, 128), f32),
                pltpu.VMEM((nb, n // 2 + n // 4, 128), f32),
                pltpu.VMEM((ni, n, 256), bf16),
                pltpu.VMEM((ni, n, 128), f32),
                pltpu.VMEM((n, 256), bf16),
                pltpu.VMEM((8, n), f32),
                pltpu.VMEM((n, 128), bf16),
                pltpu.VMEM((ni, n, 128), f32),
                pltpu.VMEM((2, ni, n // 4, 128), f32),
                pltpu.VMEM((ni, 32, 128), f32),
                pltpu.VMEM((nb, 32, 128), f32),
                dma(ni), dma(ni), dma(nb), dma(nb), dma(nb), dma(ni), dma(ni), dma(ni), dma(ni), dma(nb), dma(nb),
            ],
            compiler_params=pltpu.CompilerParams(
                collective_id=0, has_side_effects=True, vmem_limit_bytes=40 * 1024 * 1024),
        )(points, inverse_scale.reshape(1, feats), noise_var.reshape(1, n), sol, residual, direction)

    rows = P(("groups", "blk", "inner"), None)
    return jax.shard_map(
        shards, mesh=mesh,
        in_specs=(rows, P("groups"), P(("groups", "blk", "inner")), rows, rows, rows),
        out_specs=(rows, rows, rows), check_vma=False)
```

time: 224 us -> 43.3 us (0.19)
  blocking collectives: 156 us -> 0 us
  Pallas kernels: 0 us -> 37.1 us
  waiting for transfers between devices: 20.6 us -> 0 us
  matrix products: 15.5 us -> 0 us
  other arithmetic: 14.6 us -> 0 us
  between operations: 14.2 us -> 0.67 us
  local copies, waits for them, and re-layouts: 2.72 us -> 5.2 us
    psum x2 -> x0, blocking collectives: 117 us -> none  [the longest x1 59.8 us: shards(): curv, gram = lax.psum((local_curv, local_gram), ('blk', 'inner'))]
    all_gather x3 -> x0, blocking collectives: 38.3 us -> none  [the longest x1 16.3 us: shards(): lax.all_gather(scaled, 'blk', axis=0, tiled=True)]
    pallas_call x0 -> x1, Pallas kernels: none -> 37.1 us  [shards(): pl.pallas_call(functools.partial(kernel, nb, ni), out_shape=(out, out, ou...]
    reduce_scatter x1 -> x0, waiting for transfers between devices: 20.5 us -> none  [shards(): lax.psum_scatter(partial_sum, 'inner', scatter_dimension=0, tiled=True)]
    dot_general x10 -> x0, matrix products: 14.8 us -> none  [the longest x2 7.32 us: step_block(): return (acc + jnp.dot(matern(sq), block_p, precision=high), None)]
    another operation x10 -> x0, other arithmetic: 13.4 us -> none  [the longest x5 6.7 us: shards(): alpha = jax.scipy.linalg.cho_solve((jnp.linalg.cholesky(curv), True), gram)]
  transfers between devices with their start and end apart: 1 -> 0, of which waited for: 1 -> 0; matrix products, arithmetic and copies ran while one was open for 0% -> 0% of each run, Pallas kernels for 0% -> 0%
where the time goes in v1:
time: 43.3 us; the launch traced here: 43 us
  Pallas kernels  37.1 us (86%)
  local copies, waits for them, and re-layouts  5.2 us (12%)
  between operations  0.67 us (2%)
    pallas_call x1, Pallas kernels, shards(): pl.pallas_call(functools.partial(kernel, nb, ni), out_shape=(out, out, ou...  37.1 us
    unnamed x14, local copies, waits for them, and re-layouts  3.13 us
    pallas_call x3, local copies, waits for them, and re-layouts, shards(): pl.pallas_call(functools.partial(kernel, nb, ni), out_shape=(out, out, ou...  2.07 us

profile of v1, /device:TPU:0, one launch (start us, length us, event | category | flops | bytes accessed | tf_op | source)
XLA Modules:
  0.0 43.0 jit_solution(13554182355468574979)
XLA Ops:
  0.6 0.0 copy-start.2
  0.6 0.9 %copy.9.points_ref = f32[256,64]{1,0:T(8,128)S(1)} copy(f32[256,64]{0,1:T(8,128)} %param.6) | data formatting | bytes 131072 | tf_op args[0]
  1.6 0.0 copy-done.2
  1.6 0.0 copy-start.3
  1.6 0.1 copy.10.sol_ref
  1.7 0.7 %copy-done.3 = f32[256,32]{0,1:T(8,128)S(1)} copy-done((f32[256,32]{0,1:T(8,128)S(1)}, f32[256,32]{0,1:T(8,128)}, u32[]{:S(2)}) %copy-start.3) | copy-done | bytes 32792
  2.4 0.0 copy-start.4
  2.4 0.1 copy.11.res_ref
  2.5 0.7 %copy-done.4 = f32[256,32]{0,1:T(8,128)S(1)} copy-done((f32[256,32]{0,1:T(8,128)S(1)}, f32[256,32]{0,1:T(8,128)}, u32[]{:S(2)}) %copy-start.4) | copy-done | bytes 32792
  3.1 0.0 copy-start
  3.1 0.0 copy-start.1
  3.1 0.1 copy.12.dir_ref
  3.2 0.6 %copy-done = f32[256]{0:T(256)S(1)} copy-done((f32[256]{0:T(256)S(1)}, f32[256]{0:T(256)}, u32[]{:S(2)}) %copy-start) | copy-done | bytes 1048
  3.8 0.0 copy-done.1
  3.8 37.1 %shard_map.85 = (f32[256,32]{1,0:T(8,128)S(1)}, f32[256,32]{1,0:T(8,128)S(1)}, f32[256,32]{1,0:T(8,128)S(1)}) custom-call(f32[256,64]{1,0:T(8,128)S(1)} %copy.9.points_ref, f32[1,64]{1,0:T(1,128)S(1)} %bitcast.3, f32[1,256]{1,0:T(1,128)S(1)} %bitcast.2, f32[256,32]{1,0:T(8,128)S(1)} %copy.10.sol_ref, f32[256,32]{1,0:T(8,128)S(1)} %copy.11.res_ref, ...), custom_call_target="tpu_custom_call" | custom-call | tf_op jit(solution)/shard_map/pallas_call | solution.py:300
  40.9 0.7 %copy.13 = f32[256,32]{0,1:T(8,128)} copy(f32[256,32]{1,0:T(8,128)S(1)} %get-tuple-element.3) | data formatting | bytes 65536 | tf_op jit(solution)/shard_map/pallas_call | solution.py:300
  41.6 0.7 %copy.14 = f32[256,32]{0,1:T(8,128)} copy(f32[256,32]{1,0:T(8,128)S(1)} %get-tuple-element.4) | data formatting | bytes 65536 | tf_op jit(solution)/shard_map/pallas_call | solution.py:300
  42.3 0.7 %copy.15 = f32[256,32]{0,1:T(8,128)} copy(f32[256,32]{1,0:T(8,128)S(1)} %get-tuple-element.5) | data formatting | bytes 65536 | tf_op jit(solution)/shard_map/pallas_call | solution.py:300
Async XLA Ops:
  0.6 1.0 %copy-start.2 = (f32[256,32]{0,1:T(8,128)S(1)}, f32[256,32]{0,1:T(8,128)}, u32[]{:S(2)}) copy-start(f32[256,32]{0,1:T(8,128)} %param.9) | copy-start | bytes 98308
  1.6 0.8 %copy-start.3 = (f32[256,32]{0,1:T(8,128)S(1)}, f32[256,32]{0,1:T(8,128)}, u32[]{:S(2)}) copy-start(f32[256,32]{0,1:T(8,128)} %param.10) | copy-start | bytes 98308
  2.4 0.8 %copy-start.4 = (f32[256,32]{0,1:T(8,128)S(1)}, f32[256,32]{0,1:T(8,128)}, u32[]{:S(2)}) copy-start(f32[256,32]{0,1:T(8,128)} %param.11) | copy-start | bytes 98308
  3.1 0.7 %copy-start = (f32[256]{0:T(256)S(1)}, f32[256]{0:T(256)}, u32[]{:S(2)}) copy-start(f32[256]{0:T(256)} %param.8) | copy-start | bytes 3076
  3.1 0.7 %copy-start.1 = (f32[64]{0:T(128)S(1)}, f32[64]{0:T(128)}, u32[]{:S(2)}) copy-start(f32[64]{0:T(128)} %param.7) | copy-start | bytes 772

commit v2 on v0

v2 whole, which is shorter than its diff:
```python
import functools
import math

import jax
import jax.numpy as jnp
from jax import lax
from jax.experimental import pallas as pl
from jax.experimental.pallas import tpu as pltpu
from jax.sharding import PartitionSpec as P

MESH = pl.DeviceIdType.MESH
HIGH = lax.Precision.HIGHEST
LN2 = math.log(2.0)
FEATURE_SCALE = math.sqrt(5.0) / LN2
f32 = jnp.float32
bf16 = jnp.bfloat16


def dot(a, b, ca, cb, precision=HIGH):
    return lax.dot_general(a, b, (((ca,), (cb,)), ((), ())), precision=precision, preferred_element_type=f32)


def halves(x):
    hi = x.astype(bf16).astype(f32)
    lo = (x - hi).astype(bf16).astype(f32)
    return hi, lo


def row_operand(w):
    hi, lo = halves(w)
    both = jnp.concatenate([hi, lo], axis=0)
    norm = jnp.sum((hi + lo) * (hi + lo), axis=0, keepdims=True)
    both = (both.T * -2.0).astype(bf16)
    return jnp.concatenate([both, both], axis=1), jnp.broadcast_to(norm, (128, w.shape[1])).T


def col_operand(w):
    hi, lo = halves(w)
    norm = jnp.sum((hi + lo) * (hi + lo), axis=0, keepdims=True)
    hi, lo = hi.astype(bf16), lo.astype(bf16)
    return jnp.concatenate([hi, hi, lo, lo], axis=0), norm


def dir_operand(d):
    hi, lo = halves(d)
    return jnp.concatenate([hi, lo, jnp.zeros((64, d.shape[1]), f32)], axis=0).T.astype(bf16)


def eliminate(a):
    n = a.shape[0]
    rows = lax.broadcasted_iota(jnp.int32, (n, 1), 0)
    for k in range(n):
        pivot = a[k:k + 1, :] / a[k:k + 1, k:k + 1]
        column = jnp.where(rows == k, 0.0, a[:, k:k + 1])
        a = jnp.where(rows == k, pivot, a - column * pivot)
    return a[:, n:2 * n]


def kernel(nb, ni, points_hbm, scale_hbm, noise_hbm, sol_hbm, res_hbm, dir_hbm, sol_out, res_out, dir_out,
           pts, scale, noise, sol, res, wrow, cols, a_op, rn, b_op, cn, d_op, acc, parts,
           sums_i, sums_b, grams_i, grams_b, l_sem,
           w_send, w_recv, c_right, c_left, c_recv, p_send, p_recv, si_send, si_recv, sb_send, sb_recv,
           gi_send, gi_recv, gb_send, gb_recv):
    feats, n = pts.shape
    rhs = sol.shape[0]
    b = lax.axis_index("blk")
    i = lax.axis_index("inner")

    local = [
        pltpu.make_async_copy(points_hbm, pts, l_sem.at[0]),
        pltpu.make_async_copy(scale_hbm, scale, l_sem.at[1]),
        pltpu.make_async_copy(dir_hbm, cols.at[b, feats:], l_sem.at[2]),
        pltpu.make_async_copy(res_hbm, res, l_sem.at[3]),
        pltpu.make_async_copy(noise_hbm, noise, l_sem.at[4]),
        pltpu.make_async_copy(sol_hbm, sol, l_sem.at[5]),
    ]
    for copy in local:
        copy.start()

    barrier = pltpu.get_barrier_semaphore()
    for off in range(1, ni):
        pl.semaphore_signal(barrier, inc=1, device_id={"inner": lax.rem(i + off, ni)}, device_id_type=MESH)

    @pl.loop(1, nb)
    def _(off):
        pl.semaphore_signal(barrier, inc=1, device_id={"blk": lax.rem(b + off, nb)}, device_id_type=MESH)

    for copy in local:
        copy.wait()
    same = lax.broadcasted_iota(jnp.int32, (feats, feats), 0) == lax.broadcasted_iota(jnp.int32, (feats, feats), 1)
    factor = jnp.sum(jnp.where(same, scale[...] * FEATURE_SCALE, 0.0), axis=1, keepdims=True)
    own_w = pts[...] * factor
    cols[b, :feats] = own_w
    pl.semaphore_wait(barrier, ni + nb - 2)

    def w_copy(to, src):
        return pltpu.make_async_remote_copy(
            src_ref=cols.at[b, :feats], dst_ref=wrow.at[src], send_sem=w_send.at[to], recv_sem=w_recv.at[src],
            device_id={"inner": to}, device_id_type=MESH)

    def c_copy(owner, to, sems):
        return pltpu.make_async_remote_copy(
            src_ref=cols.at[owner], dst_ref=cols.at[owner], send_sem=sems.at[owner], recv_sem=c_recv.at[owner],
            device_id={"blk": to}, device_id_type=MESH)

    @pl.when(b + 1 < nb)
    def _():
        c_copy(b, b + 1, c_right).start()

    @pl.when(b >= 1)
    def _():
        c_copy(b, b - 1, c_left).start()

    for off in range(1, ni):
        w_copy(lax.rem(i + off, ni), i).start()

    def s_copy(buf, me, to, src, send, recv, axis):
        return pltpu.make_async_remote_copy(
            src_ref=buf.at[me], dst_ref=buf.at[src], send_sem=send.at[to], recv_sem=recv.at[src],
            device_id={axis: to}, device_id_type=MESH)

    def inner_send(buf, send, recv):
        for off in range(1, ni):
            s_copy(buf, i, lax.rem(i + off, ni), i, send, recv, "inner").start()

    def inner_sum(buf, send, recv):
        for off in range(1, ni):
            src = lax.rem(i - off + ni, ni)
            s_copy(buf, i, src, src, send, recv, "inner").wait_recv()
        total = buf[0]
        for j in range(1, ni):
            total = total + buf[j]
        return total

    def blk_send(buf, send, recv):
        @pl.loop(1, nb)
        def _(off):
            s_copy(buf, b, lax.rem(b + off, nb), b, send, recv, "blk").start()

    def blk_sum(buf, send, recv):
        @pl.loop(1, nb)
        def _(off):
            src = lax.rem(b - off + nb, nb)
            s_copy(buf, b, src, src, send, recv, "blk").wait_recv()
        return lax.fori_loop(1, nb, lambda j, s: s + buf[j], buf[0])

    r = res[...]
    grams_i[i] = dot(r, r, 1, 1)
    inner_send(grams_i, gi_send, gi_recv)
    acc[...] = jnp.zeros_like(acc)

    def prepare(j, w):
        op, norms = row_operand(w)
        a_op[j] = op
        rn[j] = norms

    def load_column(owner):
        op, norms = col_operand(cols[owner, :feats])
        b_op[...] = op
        cn[...] = norms
        d_op[...] = dir_operand(cols[owner, feats:])

    def tile(j):
        cross = dot(a_op[j], b_op[...], 1, 0, None)
        row_n = rn[j]
        x = cross + jnp.concatenate([row_n] * (n // 128), axis=1) + cn[...]
        x = jnp.maximum(x, 1e-30)
        v = x * lax.rsqrt(x)
        k = (1.0 + LN2 * v + (LN2 * LN2 / 3.0) * x) * jnp.exp2(-v)
        kh = k.astype(bf16)
        kl = (k - kh.astype(f32)).astype(bf16)
        return acc[j] + dot(kh, d_op[...], 1, 0, None) + dot(kl, d_op[...], 1, 0, None)

    prepare(i, own_w)
    load_column(b)

    @pl.loop(0, ni)
    def _(off):
        j = lax.rem(i - off + ni, ni)

        @pl.when(off > 0)
        def _():
            w_copy(j, j).wait_recv()
            prepare(j, wrow[j])

        acc[j] = tile(j)

    grams_b[b] = inner_sum(grams_i, gi_send, gi_recv)
    blk_send(grams_b, gb_send, gb_recv)

    reach = jnp.minimum(b, nb - 1 - b)

    def receive(t):
        near = (t + 1) // 2
        paired = b + near * (1 - 2 * (t % 2))
        far = t - reach
        single = jnp.where(2 * b > nb - 1, b - far, b + far)
        owner = jnp.where(t <= 2 * reach, paired, single)
        c_copy(owner, b, c_right).wait_recv()

        @pl.when(jnp.logical_and(owner < b, b + 1 < nb))
        def _():
            c_copy(owner, b + 1, c_right).start()

        @pl.when(jnp.logical_and(owner > b, b >= 1))
        def _():
            c_copy(owner, b - 1, c_left).start()

        load_column(owner)

    @pl.loop(1, nb - 1)
    def _(t):
        receive(t)

        @pl.loop(0, ni)
        def _(j):
            acc[j] = tile(j)

    gram = blk_sum(grams_b, gb_send, gb_recv)
    unit = (lax.broadcasted_iota(jnp.int32, (rhs, rhs), 0) == lax.broadcasted_iota(jnp.int32, (rhs, rhs), 1)).astype(f32)
    gram_inv = eliminate(jnp.concatenate([gram, unit], axis=1))

    receive(nb - 1)

    def p_copy(to, src):
        return pltpu.make_async_remote_copy(
            src_ref=parts.at[0, to], dst_ref=parts.at[1, src], send_sem=p_send.at[to], recv_sem=p_recv.at[src],
            device_id={"inner": to}, device_id_type=MESH)

    def finished(j):
        a = tile(j).T
        return a[:rhs] + a[rhs:2 * rhs]

    @pl.loop(1, ni)
    def _(off):
        to = lax.rem(i + off, ni)
        parts[0, to] = finished(to)
        p_copy(to, i).start()

    d = cols[b, feats:]
    image = finished(i) + noise[...] * d
    for off in range(1, ni):
        src = lax.rem(i - off + ni, ni)
        p_copy(src, src).wait_recv()
        image = image + parts[1, src]

    sums_i[i] = dot(image, jnp.concatenate([d, r, image], axis=0), 1, 1)
    inner_send(sums_i, si_send, si_recv)
    sums_b[b] = inner_sum(sums_i, si_send, si_recv)
    blk_send(sums_b, sb_send, sb_recv)
    total = blk_sum(sums_b, sb_send, sb_recv)

    curv, qr, qq = [total[:, rhs * g:rhs * (g + 1)] for g in range(3)]
    curv = 0.5 * (curv + curv.T)
    alpha = eliminate(jnp.concatenate([curv, gram], axis=1))
    alpha_t = alpha.T
    r_next = r - dot(alpha_t, image, 1, 0)
    change = qr - dot(qq, alpha, 1, 0)
    gram_next = gram - dot(alpha_t, qr, 1, 0).T - dot(alpha_t, change, 1, 0)
    beta = dot(gram_inv, gram_next, 1, 0)
    res_out[...] = r_next
    sol_out[...] = sol[...] + dot(alpha_t, d, 1, 0)
    dir_out[...] = r_next + dot(beta.T, d, 1, 0)

    for off in range(1, ni):
        to = lax.rem(i + off, ni)
        w_copy(to, i).wait_send()
        p_copy(to, i).wait_send()
        s_copy(sums_i, i, to, i, si_send, si_recv, "inner").wait_send()
        s_copy(grams_i, i, to, i, gi_send, gi_recv, "inner").wait_send()

    @pl.loop(1, nb)
    def _(off):
        to = lax.rem(b + off, nb)
        s_copy(sums_b, b, to, b, sb_send, sb_recv, "blk").wait_send()
        s_copy(grams_b, b, to, b, gb_send, gb_recv, "blk").wait_send()

    @pl.loop(0, nb)
    def _(o):
        @pl.when(jnp.logical_and(o <= b, b + 1 < nb))
        def _():
            c_copy(o, b, c_right).wait_send()

        @pl.when(jnp.logical_and(o >= b, b >= 1))
        def _():
            c_copy(o, b, c_left).wait_send()


def solution(mesh):
    nb, ni = mesh.shape["blk"], mesh.shape["inner"]

    def shards(points, inverse_scale, noise_var, sol, residual, direction):
        n, feats = points.shape
        rhs = direction.shape[1]
        dma = lambda k: pltpu.SemaphoreType.DMA((k,))
        vmem = pl.BlockSpec(memory_space=pltpu.VMEM)
        out = jax.ShapeDtypeStruct((rhs, n), f32)
        results = pl.pallas_call(
            functools.partial(kernel, nb, ni),
            out_shape=(out, out, out),
            in_specs=[pl.BlockSpec(memory_space=pl.ANY)] * 6,
            out_specs=(vmem, vmem, vmem),
            scratch_shapes=[
                pltpu.VMEM((feats, n), f32),
                pltpu.VMEM((1, feats), f32),
                pltpu.VMEM((1, n), f32),
                pltpu.VMEM((rhs, n), f32),
                pltpu.VMEM((rhs, n), f32),
                pltpu.VMEM((ni, feats, n), f32),
                pltpu.VMEM((nb, feats + rhs, n), f32),
                pltpu.VMEM((ni, n, 4 * feats), bf16),
                pltpu.VMEM((ni, n, 128), f32),
                pltpu.VMEM((4 * feats, n), bf16),
                pltpu.VMEM((1, n), f32),
                pltpu.VMEM((n, 128), bf16),
                pltpu.VMEM((ni, n, 128), f32),
                pltpu.VMEM((2, ni, rhs, n), f32),
                pltpu.VMEM((ni, rhs, 3 * rhs), f32),
                pltpu.VMEM((nb, rhs, 3 * rhs), f32),
                pltpu.VMEM((ni, rhs, rhs), f32),
                pltpu.VMEM((nb, rhs, rhs), f32),
                dma(6),
                dma(ni), dma(ni), dma(nb), dma(nb), dma(nb), dma(ni), dma(ni), dma(ni), dma(ni), dma(nb), dma(nb),
                dma(ni), dma(ni), dma(nb), dma(nb),
            ],
            compiler_params=pltpu.CompilerParams(
                collective_id=0, has_side_effects=True, vmem_limit_bytes=60 * 1024 * 1024),
        )(points.T, inverse_scale.reshape(1, feats), noise_var.reshape(1, n), sol.T, residual.T, direction.T)
        return tuple(x.T for x in results)

    rows = P(("groups", "blk", "inner"), None)
    return jax.shard_map(
        shards, mesh=mesh,
        in_specs=(rows, P("groups"), P(("groups", "blk", "inner")), rows, rows, rows),
        out_specs=(rows, rows, rows), check_vma=False)
```

time: 224 us -> 40.1 us (0.18)
  blocking collectives: 156 us -> 0 us
  Pallas kernels: 0 us -> 36.4 us
  waiting for transfers between devices: 20.6 us -> 0 us
  matrix products: 15.5 us -> 0 us
  other arithmetic: 14.6 us -> 0 us
  between operations: 14.2 us -> 0.65 us
    psum x2 -> x0, blocking collectives: 117 us -> none  [the longest x1 59.8 us: shards(): curv, gram = lax.psum((local_curv, local_gram), ('blk', 'inner'))]
    all_gather x3 -> x0, blocking collectives: 38.3 us -> none  [the longest x1 16.3 us: shards(): lax.all_gather(scaled, 'blk', axis=0, tiled=True)]
    pallas_call x0 -> x1, Pallas kernels: none -> 36.4 us  [shards(): pl.pallas_call(functools.partial(kernel, nb, ni), out_shape=(out, out, ou...]
    reduce_scatter x1 -> x0, waiting for transfers between devices: 20.5 us -> none  [shards(): lax.psum_scatter(partial_sum, 'inner', scatter_dimension=0, tiled=True)]
    dot_general x10 -> x0, matrix products: 14.8 us -> none  [the longest x2 7.32 us: step_block(): return (acc + jnp.dot(matern(sq), block_p, precision=high), None)]
    another operation x10 -> x0, other arithmetic: 13.4 us -> none  [the longest x5 6.7 us: shards(): alpha = jax.scipy.linalg.cho_solve((jnp.linalg.cholesky(curv), True), gram)]
  transfers between devices with their start and end apart: 1 -> 0, of which waited for: 1 -> 0; matrix products, arithmetic and copies ran while one was open for 0% -> 0% of each run, Pallas kernels for 0% -> 0%
where the time goes in v2:
time: 40.1 us; the launch traced here: 39.8 us
  Pallas kernels  36.4 us (91%)
  local copies, waits for them, and re-layouts  2.77 us (7%)
  between operations  0.65 us (2%)
    pallas_call x1, Pallas kernels, shards(): pl.pallas_call(functools.partial(kernel, nb, ni), out_shape=(out, out, ou...  36.4 us
    unnamed x7, local copies, waits for them, and re-layouts  2.77 us

profile of v2, /device:TPU:0, one launch (start us, length us, event | category | flops | bytes accessed | tf_op | source)
XLA Modules:
  0.0 39.8 jit_solution(5080273178028787318)
XLA Ops:
  0.6 36.4 %shard_map.85 = (f32[32,256]{1,0:T(8,128)}, f32[32,256]{1,0:T(8,128)}, f32[32,256]{1,0:T(8,128)}) custom-call(f32[64,256]{1,0:T(8,128)} %bitcast.9, f32[1,64]{1,0:T(1,128)} %bitcast.17, f32[1,256]{1,0:T(1,128)} %bitcast.16, f32[32,256]{1,0:T(8,128)} %bitcast.10, f32[32,256]{1,0:T(8,128)} %bitcast.11, f32[32,256]{1,0:T(8,128)} %bitcast.12), custom_call_target="tpu_custom_call" | custom-call | tf_op jit(solution)/shard_map/pallas_call | solution.py:298
  37.0 0.0 copy-start.1
  37.0 1.4 %copy.12 = f32[256,32]{0,1:T(8,128)} copy(f32[256,32]{0,1:T(8,128)} %bitcast.15) | data formatting | bytes 65536
  38.4 0.0 copy-done.1
  38.4 0.0 copy-start
  38.4 0.6 %copy.13 = f32[256,32]{0,1:T(8,128)} copy(f32[256,32]{0,1:T(8,128)S(1)} %bitcast.14) | data formatting | bytes 65536
  39.0 0.2 copy-done
  39.2 0.6 %copy.14 = f32[256,32]{0,1:T(8,128)} copy(f32[256,32]{0,1:T(8,128)S(1)} %bitcast.13) | data formatting | bytes 65536
Async XLA Ops:
  37.0 1.4 %copy-start.1 = (f32[32,256]{1,0:T(8,128)S(1)}, f32[32,256]{1,0:T(8,128)}, u32[]{:S(2)}) copy-start(f32[32,256]{1,0:T(8,128)} %get-tuple-element.7) | copy-start | bytes 98308
  38.4 0.8 %copy-start = (f32[32,256]{1,0:T(8,128)S(1)}, f32[32,256]{1,0:T(8,128)}, u32[]{:S(2)}) copy-start(f32[32,256]{1,0:T(8,128)} %get-tuple-element.8) | copy-start | bytes 98308

commit v3 on v2

--- a/solution.py
+++ b/solution.py
@@ -46,21 +46,36 @@
     return jnp.concatenate([hi, lo, jnp.zeros((64, d.shape[1]), f32)], axis=0).T.astype(bf16)
 
 
-def eliminate(a):
-    n = a.shape[0]
-    rows = lax.broadcasted_iota(jnp.int32, (n, 1), 0)
-    for k in range(n):
-        pivot = a[k:k + 1, :] / a[k:k + 1, k:k + 1]
-        column = jnp.where(rows == k, 0.0, a[:, k:k + 1])
-        a = jnp.where(rows == k, pivot, a - column * pivot)
-    return a[:, n:2 * n]
+def eliminate(a, first, last):
+    rows = lax.broadcasted_iota(jnp.int32, (a.shape[0], 1), 0)
+    for k in range(first, last, 2):
+        r0, r1 = a[k:k + 1, :], a[k + 1:k + 2, :]
+        c0, c1 = a[:, k:k + 1], a[:, k + 1:k + 2]
+        p01 = a[k:k + 1, k + 1:k + 2]
+        inv0 = 1.0 / a[k:k + 1, k:k + 1]
+        low = a[k + 1:k + 2, k:k + 1] * inv0
+        inv1 = 1.0 / (a[k + 1:k + 2, k + 1:k + 2] - low * p01)
+        r1 = (r1 - low * r0) * inv1
+        r0 = (r0 - p01 * r1) * inv0
+        a = jnp.where(rows == k, r0, jnp.where(rows == k + 1, r1, a - c0 * r0 - c1 * r1))
+    return a
+
+
+def pack4(x):
+    n = x.shape[0] // 4
+    return jnp.concatenate([x[g * n:(g + 1) * n] for g in range(4)], axis=1)
+
+
+def unpack4(x):
+    n = x.shape[1] // 4
+    return jnp.concatenate([x[:, g * n:(g + 1) * n] for g in range(4)], axis=0)
 
 
 def kernel(nb, ni, points_hbm, scale_hbm, noise_hbm, sol_hbm, res_hbm, dir_hbm, sol_out, res_out, dir_out,
            pts, scale, noise, sol, res, wrow, cols, a_op, rn, b_op, cn, d_op, acc, parts,
-           sums_i, sums_b, grams_i, grams_b, l_sem,
+           sums_i, sums_b, grams_i, grams_b, curv_i, curv_b, l_sem,
            w_send, w_recv, c_right, c_left, c_recv, p_send, p_recv, si_send, si_recv, sb_send, sb_recv,
-           gi_send, gi_recv, gb_send, gb_recv):
+           gi_send, gi_recv, gb_send, gb_recv, ci_send, ci_recv, cb_send, cb_recv):
     feats, n = pts.shape
     rhs = sol.shape[0]
     b = lax.axis_index("blk")
@@ -145,7 +160,7 @@
         return lax.fori_loop(1, nb, lambda j, s: s + buf[j], buf[0])
 
     r = res[...]
-    grams_i[i] = dot(r, r, 1, 1)
+    grams_i[i] = pack4(dot(r, r, 1, 1))
     inner_send(grams_i, gi_send, gi_recv)
     acc[...] = jnp.zeros_like(acc)
 
@@ -216,9 +231,6 @@
         def _(j):
             acc[j] = tile(j)
 
-    gram = blk_sum(grams_b, gb_send, gb_recv)
-    unit = (lax.broadcasted_iota(jnp.int32, (rhs, rhs), 0) == lax.broadcasted_iota(jnp.int32, (rhs, rhs), 1)).astype(f32)
-    gram_inv = eliminate(jnp.concatenate([gram, unit], axis=1))
 
     receive(nb - 1)
 
@@ -244,19 +256,28 @@
         p_copy(src, src).wait_recv()
         image = image + parts[1, src]
 
-    sums_i[i] = dot(image, jnp.concatenate([d, r, image], axis=0), 1, 1)
+    curv_i[i] = pack4(dot(d, image, 1, 1))
+    inner_send(curv_i, ci_send, ci_recv)
+    rest = dot(jnp.concatenate([r, image], axis=0), image, 1, 1)
+    sums_i[i] = pack4(rest)
     inner_send(sums_i, si_send, si_recv)
+    gram = unpack4(blk_sum(grams_b, gb_send, gb_recv))
+    unit = (lax.broadcasted_iota(jnp.int32, (rhs, rhs), 0) == lax.broadcasted_iota(jnp.int32, (rhs, rhs), 1)).astype(f32)
+    inverse = eliminate(jnp.concatenate([gram, unit], axis=1), 0, rhs // 2)
+    curv_b[b] = inner_sum(curv_i, ci_send, ci_recv)
+    blk_send(curv_b, cb_send, cb_recv)
     sums_b[b] = inner_sum(sums_i, si_send, si_recv)
     blk_send(sums_b, sb_send, sb_recv)
-    total = blk_sum(sums_b, sb_send, sb_recv)
-
-    curv, qr, qq = [total[:, rhs * g:rhs * (g + 1)] for g in range(3)]
+    gram_inv = eliminate(inverse, rhs // 2, rhs)[:, rhs:]
+    curv = unpack4(blk_sum(curv_b, cb_send, cb_recv))
     curv = 0.5 * (curv + curv.T)
-    alpha = eliminate(jnp.concatenate([curv, gram], axis=1))
+    alpha = eliminate(jnp.concatenate([curv, gram], axis=1), 0, rhs)[:, rhs:]
+    rest = unpack4(blk_sum(sums_b, sb_send, sb_recv))
+    rq, qq = rest[:rhs], rest[rhs:]
     alpha_t = alpha.T
     r_next = r - dot(alpha_t, image, 1, 0)
-    change = qr - dot(qq, alpha, 1, 0)
-    gram_next = gram - dot(alpha_t, qr, 1, 0).T - dot(alpha_t, change, 1, 0)
+    change = rq.T - dot(qq, alpha, 1, 0)
+    gram_next = gram - dot(rq, alpha, 1, 0) - dot(alpha_t, change, 1, 0)
     beta = dot(gram_inv, gram_next, 1, 0)
     res_out[...] = r_next
     sol_out[...] = sol[...] + dot(alpha_t, d, 1, 0)
@@ -268,12 +289,14 @@
         p_copy(to, i).wait_send()
         s_copy(sums_i, i, to, i, si_send, si_recv, "inner").wait_send()
         s_copy(grams_i, i, to, i, gi_send, gi_recv, "inner").wait_send()
+        s_copy(curv_i, i, to, i, ci_send, ci_recv, "inner").wait_send()
 
     @pl.loop(1, nb)
     def _(off):
         to = lax.rem(b + off, nb)
         s_copy(sums_b, b, to, b, sb_send, sb_recv, "blk").wait_send()
         s_copy(grams_b, b, to, b, gb_send, gb_recv, "blk").wait_send()
+        s_copy(curv_b, b, to, b, cb_send, cb_recv, "blk").wait_send()
 
     @pl.loop(0, nb)
     def _(o):
@@ -284,6 +307,14 @@
         @pl.when(jnp.logical_and(o >= b, b >= 1))
         def _():
             c_copy(o, b, c_left).wait_send()
+
+
+def write_out(a, b, c, a_out, b_out, c_out, sems):
+    copies = [pltpu.make_async_copy(x, y, sems.at[k]) for k, (x, y) in enumerate(((a, a_out), (b, b_out), (c, c_out)))]
+    for copy in copies:
+        copy.start()
+    for copy in copies:
+        copy.wait()
 
 
 def solution(mesh):
@@ -298,7 +329,7 @@
         results = pl.pallas_call(
             functools.partial(kernel, nb, ni),
             out_shape=(out, out, out),
-            in_specs=[pl.BlockSpec(memory_space=pl.ANY)] * 6,
+            in_specs=[pl.BlockSpec(memory_space=pltpu.HBM)] * 6,
             out_specs=(vmem, vmem, vmem),
             scratch_shapes=[
                 pltpu.VMEM((feats, n), f32),
@@ -315,17 +346,22 @@
                 pltpu.VMEM((n, 128), bf16),
                 pltpu.VMEM((ni, n, 128), f32),
                 pltpu.VMEM((2, ni, rhs, n), f32),
-                pltpu.VMEM((ni, rhs, 3 * rhs), f32),
-                pltpu.VMEM((nb, rhs, 3 * rhs), f32),
-                pltpu.VMEM((ni, rhs, rhs), f32),
-                pltpu.VMEM((nb, rhs, rhs), f32),
+                pltpu.VMEM((ni, rhs // 2, 4 * rhs), f32),
+                pltpu.VMEM((nb, rhs // 2, 4 * rhs), f32),
+                pltpu.VMEM((ni, rhs // 4, 4 * rhs), f32),
+                pltpu.VMEM((nb, rhs // 4, 4 * rhs), f32),
+                pltpu.VMEM((ni, rhs // 4, 4 * rhs), f32),
+                pltpu.VMEM((nb, rhs // 4, 4 * rhs), f32),
                 dma(6),
                 dma(ni), dma(ni), dma(nb), dma(nb), dma(nb), dma(ni), dma(ni), dma(ni), dma(ni), dma(nb), dma(nb),
-                dma(ni), dma(ni), dma(nb), dma(nb),
+                dma(ni), dma(ni), dma(nb), dma(nb), dma(ni), dma(ni), dma(nb), dma(nb),
             ],
             compiler_params=pltpu.CompilerParams(
                 collective_id=0, has_side_effects=True, vmem_limit_bytes=60 * 1024 * 1024),
         )(points.T, inverse_scale.reshape(1, feats), noise_var.reshape(1, n), sol.T, residual.T, direction.T)
+        results = pl.pallas_call(
+            write_out, out_shape=(out, out, out), in_specs=[vmem] * 3,
+            out_specs=[pl.BlockSpec(memory_space=pltpu.HBM)] * 3, scratch_shapes=[dma(3)])(*results)
         return tuple(x.T for x in results)
 
     rows = P(("groups", "blk", "inner"), None)

time: 40.1 us -> 36.7 us (0.915)
  local copies, waits for them, and re-layouts: 2.77 us -> 0 us
  Pallas kernels: 36.4 us -> 35.8 us
    unnamed x7 -> x0, local copies, waits for them, and re-layouts: 2.77 us -> none
    pallas_call x1, Pallas kernels: 36.4 us -> 34.4 us  [shards(): pl.pallas_call(functools.partial(kernel, nb, ni), out_shape=(out, out, ou...]
    pallas_call x0 -> x1, Pallas kernels: none -> 1.45 us  [shards(): pl.pallas_call(write_out, out_shape=(out, out, out), in_specs=[vmem] * 3,...]
where the time goes in v3:
time: 36.7 us; the launch traced here: 36.5 us
  Pallas kernels  35.8 us (98%)
  between operations  0.64 us (2%)
    pallas_call x1, Pallas kernels, shards(): pl.pallas_call(functools.partial(kernel, nb, ni), out_shape=(out, out, ou...  34.4 us
    pallas_call x1, Pallas kernels, shards(): pl.pallas_call(write_out, out_shape=(out, out, out), in_specs=[vmem] * 3,...  1.45 us

profile of v3, /device:TPU:0, one launch (start us, length us, event | category | flops | bytes accessed | tf_op | source)
XLA Modules:
  0.0 36.5 jit_solution(2832984146400639019)
XLA Ops:
  0.6 34.4 %shard_map.85 = (f32[32,256]{1,0:T(8,128)}, f32[32,256]{1,0:T(8,128)}, f32[32,256]{1,0:T(8,128)}) custom-call(f32[64,256]{1,0:T(8,128)} %bitcast.9, f32[1,64]{1,0:T(1,128)} %bitcast.14, f32[1,256]{1,0:T(1,128)} %bitcast.13, f32[32,256]{1,0:T(8,128)} %bitcast.10, f32[32,256]{1,0:T(8,128)} %bitcast.11, f32[32,256]{1,0:T(8,128)} %bitcast.12), custom_call_target="tpu_custom_call" | custom-call | tf_op jit(solution)/shard_map/pallas_call | solution.py:329
  35.0 1.5 %shard_map.86 = (f32[32,256]{1,0:T(8,128)}, f32[32,256]{1,0:T(8,128)}, f32[32,256]{1,0:T(8,128)}) custom-call(f32[32,256]{1,0:T(8,128)} %get-tuple-element.9.a, f32[32,256]{1,0:T(8,128)} %get-tuple-element.10.b, f32[32,256]{1,0:T(8,128)} %get-tuple-element.11.c), custom_call_target="tpu_custom_call" | custom-call | tf_op jit(solution)/shard_map/pallas_call | solution.py:362

commit v4 on v3

--- a/solution.py
+++ b/solution.py
@@ -74,7 +74,7 @@
 def kernel(nb, ni, points_hbm, scale_hbm, noise_hbm, sol_hbm, res_hbm, dir_hbm, sol_out, res_out, dir_out,
            pts, scale, noise, sol, res, wrow, cols, a_op, rn, b_op, cn, d_op, acc, parts,
            sums_i, sums_b, grams_i, grams_b, curv_i, curv_b, l_sem,
-           w_send, w_recv, c_right, c_left, c_recv, p_send, p_recv, si_send, si_recv, sb_send, sb_recv,
+           w_send, w_recv, c_send, c_recv, p_send, p_recv, si_send, si_recv, sb_send, sb_recv,
            gi_send, gi_recv, gb_send, gb_recv, ci_send, ci_recv, cb_send, cb_recv):
     feats, n = pts.shape
     rhs = sol.shape[0]
@@ -113,18 +113,23 @@
             src_ref=cols.at[b, :feats], dst_ref=wrow.at[src], send_sem=w_send.at[to], recv_sem=w_recv.at[src],
             device_id={"inner": to}, device_id_type=MESH)
 
-    def c_copy(owner, to, sems):
+    def c_copy(to, owner):
         return pltpu.make_async_remote_copy(
-            src_ref=cols.at[owner], dst_ref=cols.at[owner], send_sem=sems.at[owner], recv_sem=c_recv.at[owner],
+            src_ref=cols.at[owner], dst_ref=cols.at[owner], send_sem=c_send.at[to], recv_sem=c_recv.at[owner],
             device_id={"blk": to}, device_id_type=MESH)
 
-    @pl.when(b + 1 < nb)
-    def _():
-        c_copy(b, b + 1, c_right).start()
-
-    @pl.when(b >= 1)
-    def _():
-        c_copy(b, b - 1, c_left).start()
+    reach = jnp.minimum(b, nb - 1 - b)
+
+    def owner_at(t):
+        near = (t + 1) // 2
+        paired = b + near * (1 - 2 * (t % 2))
+        far = t - reach
+        single = jnp.where(2 * b > nb - 1, b - far, b + far)
+        return jnp.where(t <= 2 * reach, paired, single)
+
+    @pl.loop(1, nb)
+    def _(t):
+        c_copy(owner_at(t), b).start()
 
     for off in range(1, ni):
         w_copy(lax.rem(i + off, ni), i).start()
@@ -203,31 +208,16 @@
     grams_b[b] = inner_sum(grams_i, gi_send, gi_recv)
     blk_send(grams_b, gb_send, gb_recv)
 
-    reach = jnp.minimum(b, nb - 1 - b)
-
     def receive(t):
-        near = (t + 1) // 2
-        paired = b + near * (1 - 2 * (t % 2))
-        far = t - reach
-        single = jnp.where(2 * b > nb - 1, b - far, b + far)
-        owner = jnp.where(t <= 2 * reach, paired, single)
-        c_copy(owner, b, c_right).wait_recv()
-
-        @pl.when(jnp.logical_and(owner < b, b + 1 < nb))
-        def _():
-            c_copy(owner, b + 1, c_right).start()
-
-        @pl.when(jnp.logical_and(owner > b, b >= 1))
-        def _():
-            c_copy(owner, b - 1, c_left).start()
-
+        owner = owner_at(t)
+        c_copy(owner, owner).wait_recv()
         load_column(owner)
 
     @pl.loop(1, nb - 1)
     def _(t):
         receive(t)
 
-        @pl.loop(0, ni)
+        @pl.loop(0, ni, unroll=ni)
         def _(j):
             acc[j] = tile(j)
 
@@ -243,7 +233,7 @@
         a = tile(j).T
         return a[:rhs] + a[rhs:2 * rhs]
 
-    @pl.loop(1, ni)
+    @pl.loop(1, ni, unroll=ni - 1)
     def _(off):
         to = lax.rem(i + off, ni)
         parts[0, to] = finished(to)
@@ -273,12 +263,13 @@
     curv = 0.5 * (curv + curv.T)
     alpha = eliminate(jnp.concatenate([curv, gram], axis=1), 0, rhs)[:, rhs:]
     rest = unpack4(blk_sum(sums_b, sb_send, sb_recv))
-    rq, qq = rest[:rhs], rest[rhs:]
+    rq = rest[:rhs]
     alpha_t = alpha.T
     r_next = r - dot(alpha_t, image, 1, 0)
-    change = rq.T - dot(qq, alpha, 1, 0)
-    gram_next = gram - dot(rq, alpha, 1, 0) - dot(alpha_t, change, 1, 0)
-    beta = dot(gram_inv, gram_next, 1, 0)
+    moved = dot(rest, alpha, 1, 0)
+    change = rq.T - moved[rhs:]
+    inv_alpha = dot(gram_inv, alpha_t, 1, 0)
+    beta = unit - dot(gram_inv, moved[:rhs], 1, 0) - dot(inv_alpha, change, 1, 0)
     res_out[...] = r_next
     sol_out[...] = sol[...] + dot(alpha_t, d, 1, 0)
     dir_out[...] = r_next + dot(beta.T, d, 1, 0)
@@ -297,16 +288,7 @@
         s_copy(sums_b, b, to, b, sb_send, sb_recv, "blk").wait_send()
         s_copy(grams_b, b, to, b, gb_send, gb_recv, "blk").wait_send()
         s_copy(curv_b, b, to, b, cb_send, cb_recv, "blk").wait_send()
-
-    @pl.loop(0, nb)
-    def _(o):
-        @pl.when(jnp.logical_and(o <= b, b + 1 < nb))
-        def _():
-            c_copy(o, b, c_right).wait_send()
-
-        @pl.when(jnp.logical_and(o >= b, b >= 1))
-        def _():
-            c_copy(o, b, c_left).wait_send()
+        c_copy(to, b).wait_send()
 
 
 def write_out(a, b, c, a_out, b_out, c_out, sems):
@@ -353,7 +335,7 @@
                 pltpu.VMEM((ni, rhs // 4, 4 * rhs), f32),
                 pltpu.VMEM((nb, rhs // 4, 4 * rhs), f32),
                 dma(6),
-                dma(ni), dma(ni), dma(nb), dma(nb), dma(nb), dma(ni), dma(ni), dma(ni), dma(ni), dma(nb), dma(nb),
+                dma(ni), dma(ni), dma(nb), dma(nb), dma(ni), dma(ni), dma(ni), dma(ni), dma(nb), dma(nb),
                 dma(ni), dma(ni), dma(nb), dma(nb), dma(ni), dma(ni), dma(nb), dma(nb),
             ],
             compiler_params=pltpu.CompilerParams(

time: 36.7 us -> 34.8 us (0.948)
  Pallas kernels: 35.8 us -> 34 us
    pallas_call x1, Pallas kernels: 34.4 us -> 32.5 us  [shards(): pl.pallas_call(functools.partial(kernel, nb, ni), out_shape=(out, out, ou...]
where the time goes in v4:
time: 34.8 us; the launch traced here: 34.6 us
  Pallas kernels  34 us (98%)
  between operations  0.64 us (2%)
    pallas_call x1, Pallas kernels, shards(): pl.pallas_call(functools.partial(kernel, nb, ni), out_shape=(out, out, ou...  32.5 us
    pallas_call x1, Pallas kernels, shards(): pl.pallas_call(write_out, out_shape=(out, out, out), in_specs=[vmem] * 3,...  1.45 us

profile of v4, /device:TPU:0, one launch (start us, length us, event | category | flops | bytes accessed | tf_op | source)
XLA Modules:
  0.0 34.6 jit_solution(11798199702181739432)
XLA Ops:
  0.6 32.5 %shard_map.85 = (f32[32,256]{1,0:T(8,128)}, f32[32,256]{1,0:T(8,128)}, f32[32,256]{1,0:T(8,128)}) custom-call(f32[64,256]{1,0:T(8,128)} %bitcast.9, f32[1,64]{1,0:T(1,128)} %bitcast.14, f32[1,256]{1,0:T(1,128)} %bitcast.13, f32[32,256]{1,0:T(8,128)} %bitcast.10, f32[32,256]{1,0:T(8,128)} %bitcast.11, f32[32,256]{1,0:T(8,128)} %bitcast.12), custom_call_target="tpu_custom_call" | custom-call | tf_op jit(solution)/shard_map/pallas_call | solution.py:311
  33.1 1.5 %shard_map.86 = (f32[32,256]{1,0:T(8,128)}, f32[32,256]{1,0:T(8,128)}, f32[32,256]{1,0:T(8,128)}) custom-call(f32[32,256]{1,0:T(8,128)} %get-tuple-element.9.a, f32[32,256]{1,0:T(8,128)} %get-tuple-element.10.b, f32[32,256]{1,0:T(8,128)} %get-tuple-element.11.c), custom_call_target="tpu_custom_call" | custom-call | tf_op jit(solution)/shard_map/pallas_call | solution.py:344

commit v5 on v4

--- a/solution.py
+++ b/solution.py
@@ -100,7 +100,7 @@
     def _(off):
         pl.semaphore_signal(barrier, inc=1, device_id={"blk": lax.rem(b + off, nb)}, device_id_type=MESH)
 
-    for copy in local:
+    for copy in local[:3]:
         copy.wait()
     same = lax.broadcasted_iota(jnp.int32, (feats, feats), 0) == lax.broadcasted_iota(jnp.int32, (feats, feats), 1)
     factor = jnp.sum(jnp.where(same, scale[...] * FEATURE_SCALE, 0.0), axis=1, keepdims=True)
@@ -164,6 +164,7 @@
             s_copy(buf, b, src, src, send, recv, "blk").wait_recv()
         return lax.fori_loop(1, nb, lambda j, s: s + buf[j], buf[0])
 
+    local[3].wait()
     r = res[...]
     grams_i[i] = pack4(dot(r, r, 1, 1))
     inner_send(grams_i, gi_send, gi_recv)
@@ -239,6 +240,8 @@
         parts[0, to] = finished(to)
         p_copy(to, i).start()
 
+    local[4].wait()
+    local[5].wait()
     d = cols[b, feats:]
     image = finished(i) + noise[...] * d
     for off in range(1, ni):

time: 34.8 us -> 34.8 us (level)
  no operation moved by 1% of the time
where the time goes in v5:
time: 34.8 us; the launch traced here: 34.6 us
  Pallas kernels  34 us (98%)
  between operations  0.64 us (2%)
    pallas_call x1, Pallas kernels, shards(): pl.pallas_call(functools.partial(kernel, nb, ni), out_shape=(out, out, ou...  32.5 us
    pallas_call x1, Pallas kernels, shards(): pl.pallas_call(write_out, out_shape=(out, out, out), in_specs=[vmem] * 3,...  1.45 us

profile of v5, /device:TPU:0, one launch (start us, length us, event | category | flops | bytes accessed | tf_op | source)
XLA Modules:
  0.0 34.6 jit_solution(12486870979770414314)
XLA Ops:
  0.6 32.5 %shard_map.85 = (f32[32,256]{1,0:T(8,128)}, f32[32,256]{1,0:T(8,128)}, f32[32,256]{1,0:T(8,128)}) custom-call(f32[64,256]{1,0:T(8,128)} %bitcast.9, f32[1,64]{1,0:T(1,128)} %bitcast.14, f32[1,256]{1,0:T(1,128)} %bitcast.13, f32[32,256]{1,0:T(8,128)} %bitcast.10, f32[32,256]{1,0:T(8,128)} %bitcast.11, f32[32,256]{1,0:T(8,128)} %bitcast.12), custom_call_target="tpu_custom_call" | custom-call | tf_op jit(solution)/shard_map/pallas_call | solution.py:314
  33.2 1.5 %shard_map.86 = (f32[32,256]{1,0:T(8,128)}, f32[32,256]{1,0:T(8,128)}, f32[32,256]{1,0:T(8,128)}) custom-call(f32[32,256]{1,0:T(8,128)} %get-tuple-element.9.a, f32[32,256]{1,0:T(8,128)} %get-tuple-element.10.b, f32[32,256]{1,0:T(8,128)} %get-tuple-element.11.c), custom_call_target="tpu_custom_call" | custom-call | tf_op jit(solution)/shard_map/pallas_call | solution.py:347
